TPU v7x, 768 devices: a whole 4x8x12 slice. The times are simulated.
768 devices in a mesh: ab: 64 (over y, x, z_hi), cd: 12 (over z_lo, core).
Axes of the slice: x: 4, y: 8, z: 12 (z_hi: 2, z_lo: 6; z = z_hi * 6 + z_lo), core: 2. Of those that a mesh axis runs over, the one named last changes fastest.
Arguments:
- integrals: bfloat16 [32768, 12, 1024], P('ab', 'cd'), may hold values from -0.15625 to 0.15625
- amplitudes: bfloat16 [12, 1024, 3072], P('cd', 'ab'), may hold values from -6 to 6
- cd_irrep: int32 [12, 1024], P('cd', 'ab'), may hold values from 0 to 7, as said below
- residual: bfloat16 [32768, 3072], P('ab', 'cd'), may hold values from -6 to 6
- ab_energy: float32 [32768], P('ab'), may hold values from 1 to 4
- ij_energy: float32 [3072], P('cd'), may hold values from -2 to -0.5
Outputs:
- updated: bfloat16 [32768, 3072], P('ab', 'cd')
Inputs may be any that keep to these rules, and one draw needn't show every extreme that they name: `cd_irrep`: values 0 to 7. In each aligned piece of 16 pairs of a slab at most 4 pairs have label 0, and every piece has at least one. In at least half of the slabs (rounded up) every piece has exactly 4.
All inputs are finite; a program needn't handle non-finite values.
Results may differ from a plain program's by a relative error of at most 0.018.
Values may be sent and summed in bfloat16 or wider, within the bound.
A program may use at most 32 MiB of HBM per device.

v0:
```python
import jax
import jax.numpy as jnp
from jax import lax
from jax.sharding import PartitionSpec as P


def local(integrals, amplitudes, cd_irrep, residual, ab_energy, ij_energy):
    block = integrals[:, 0, :]
    local_rows = amplitudes[0]
    labels = cd_irrep[0]
    keep_mask = (labels == 0).astype(jnp.bfloat16)
    masked = local_rows * keep_mask[:, None]
    slab_total = jnp.dot(
        block, lax.all_gather(masked, "ab", axis=0, tiled=True), preferred_element_type=jnp.float32
    )
    ladder = lax.psum_scatter(
        slab_total.astype(jnp.bfloat16), "cd", scatter_dimension=1, tiled=True
    ).astype(jnp.float32)
    denominator = ab_energy[:, None] - ij_energy[None, :]
    return ((residual.astype(jnp.float32) + ladder) / denominator).astype(jnp.bfloat16)


def solution(mesh):
    return jax.shard_map(
        local,
        mesh=mesh,
        in_specs=(
            P("ab", "cd", None),
            P("cd", "ab", None),
            P("cd", "ab"),
            P("ab", "cd"),
            P("ab"),
            P("cd"),
        ),
        out_specs=P("ab", "cd"),
        check_vma=False,
    )
```

profile of v0, /device:TPU:1, one launch (start us, length us, event | category | flops | bytes accessed | tf_op | source)
XLA Modules:
  0.0 320.5 jit_solution(17485153969348575606)
XLA Ops:
  6.5 0.0 copy-start
  6.5 0.0 all-gather.2.cloned.1.call-start
  6.5 0.7 fusion.2
  7.3 1.6 bitcast_multiply_fusion
  8.9 0.0 all-gather.2.cloned.1.call-update
  8.9 0.0 copy-start.1
  8.9 0.0 copy-start.2
  8.9 0.0 copy-start.3
  9.0 0.0 reduce-scatter.2.cloned.1.call-start
  9.0 225.5 %all-gather.2.cloned.1.call-done = bf16[1024,3072]{1,0:T(8,128)(2,1)} async-done(((bf16[16,3072]{1,0:T(8,128)(2,1)}), bf16[1024,3072]{1,0:T(8,128)(2,1)}) %all-gather.2.cloned.1.call-update) | async-done | bytes 6291472 | tf_op jit(solution)/shard_map/all_gather | solution.py:14
  234.5 0.0 copy-done
  234.5 7.8 %fusion = bf16[512,3072]{0,1:T(8,128)(2,1)} fusion(bf16[1024,3072]{1,0:T(8,128)(2,1)} %all-gather.2.cloned.1.call-done, bf16[512,1,1024]{2,0,1:T(8,128)(2,1)S(1)} %copy-done), kind=kOutput, calls=%fused_computation.1 | convolution fusion | flops 3222798336 | bytes 10485760 | tf_op jit(solution)/shard_map/dot_general | solution.py:13
  242.3 0.0 reduce-scatter.2.cloned.1.call-update
  242.3 0.0 copy-done.1
  242.3 0.1 copy.7
  242.4 69.3 %reduce-scatter.2.cloned.1.call-done = bf16[512,256]{0,1:T(8,128)(2,1)} async-done(((bf16[512,3072]{0,1:T(8,128)(2,1)}), bf16[512,256]{0,1:T(8,128)(2,1)}) %reduce-scatter.2.cloned.1.call-update) | async-done | bytes 262160 | tf_op jit(solution)/shard_map/reduce_scatter | solution.py:16
  311.7 0.0 copy-done.2
  311.7 0.0 copy-done.3
  311.7 1.1 divide_convert_fusion
  312.8 0.8 copy.8
Async XLA Ops:
  6.5 227.9 %copy-start = (bf16[512,1,1024]{2,0,1:T(8,128)(2,1)S(1)}, bf16[512,1,1024]{2,0,1:T(8,128)(2,1)}, u32[]{:S(2)}) copy-start(bf16[512,1,1024]{2,0,1:T(8,128)(2,1)} %param.6) | copy-start | bytes 3145732
  6.5 227.9 %all-gather.2.cloned.1.call-start = ((), (), s32[]{:S(2)}) async-start(), calls=%async_computation.1 | async-start | bytes 6389760 | tf_op jit(solution)/shard_map/all_gather | solution.py:14
  8.9 233.4 %copy-start.1 = (bf16[512,256]{1,0:T(8,128)(2,1)S(1)}, bf16[512,256]{1,0:T(8,128)(2,1)}, u32[]{:S(2)}) copy-start(bf16[512,256]{1,0:T(8,128)(2,1)} %param.9) | copy-start | bytes 786436
  8.9 302.8 %copy-start.2 = (f32[512]{0:T(512)S(1)}, f32[512]{0:T(512)}, u32[]{:S(2)}) copy-start(f32[512]{0:T(512)} %param.10) | copy-start | bytes 6148
  8.9 302.8 %copy-start.3 = (f32[256]{0:T(256)S(1)}, f32[256]{0:T(256)}, u32[]{:S(2)}) copy-start(f32[256]{0:T(256)} %param.11) | copy-start | bytes 3076
  9.0 302.8 %reduce-scatter.2.cloned.1.call-start = ((), (), s32[]{:S(2)}) async-start(), calls=%async_computation.2 | async-start | bytes 3407872 | tf_op jit(solution)/shard_map/reduce_scatter | solution.py:16
Sparse Core Ops, SparseCore 0:
  12.7 221.7 all-gather.1
  242.4 69.2 reduce-scatter.1
where the time goes:
time: 325 us; the launch traced here: 321 us
  waiting for transfers between devices  295 us (91%)
  between operations  13.4 us (4%)
  matrix products  7.8 us (2%)
  other arithmetic  3.45 us (1%)
    all_gather x1, waiting for transfers between devices, local(): lax.all_gather(masked, 'ab', axis=0, tiled=True)  225 us
    reduce_scatter x1, waiting for transfers between devices, local(): lax.psum_scatter(slab_total.astype(jnp.bfloat16), 'cd', scatter_dimension...  69.3 us
    dot_general x1, matrix products, local(): jnp.dot(block, lax.all_gather(masked, 'ab', axis=0, tiled=True), preferre...  7.8 us
  transfers between devices with their start and end apart: 2, of which 2 were waited for; matrix products, arithmetic and copies ran while one was open for 0% of the time, Pallas kernels for 0%

commit v1 on v0

v1 whole, which is shorter than its diff:
```python
import jax
import jax.numpy as jnp
from jax import lax
from jax.experimental import pallas as pl
from jax.experimental.pallas import tpu as pltpu
from jax.sharding import PartitionSpec as P

MESH = pl.DeviceIdType.MESH
NX, NY, NZ = 4, 8, 6
F32, BF16 = jnp.float32, jnp.bfloat16


def iota(shape, dim):
    return lax.broadcasted_iota(jnp.int32, shape, dim)


def kernel(
    v_hbm, t_hbm, lab_hbm, res_hbm, ab_hbm, ij_hbm,
    out_ref,
    lab, t_in, v_in, res, abe, ije, den,
    lx, ly, lz, tsend, tx, ty, vb, acc, xs, xr,
    loc, lxs, lxr, lys, lyr, lzs, tzs, tzr, txs, txr, tys, tyr, vs, vr, cs, late_in,
):
    ab, cd = lax.axis_index("ab"), lax.axis_index("cd")
    y, x, zh = ab // 8, (ab // 2) % 4, ab % 2
    zl, c = cd // 2, cd % 2

    def dev(yy=y, xx=x, hh=zh, ll=zl, cc=c):
        return ((yy * NX + xx) * 2 + hh, ll * 2 + cc)

    def rc(src, dst, ss, rs, to):
        return pltpu.make_async_remote_copy(
            src_ref=src, dst_ref=dst, send_sem=ss, recv_sem=rs, device_id=to, device_id_type=MESH
        )

    def xat(d):
        return lax.rem(x + d + NX, NX)

    def yat(d):
        return lax.rem(y + d + NY, NY)

    loads = [
        pltpu.make_async_copy(a, b, loc.at[i])
        for i, (a, b) in enumerate(
            [(lab_hbm, lab), (t_hbm, t_in), (v_hbm, v_in), (res_hbm, res), (ab_hbm, abe), (ij_hbm, ije)]
        )
    ]
    for cp in loads:
        cp.start()

    barrier = pltpu.get_barrier_semaphore()

    def hello(to):
        pl.semaphore_signal(barrier, inc=1, device_id=to, device_id_type=MESH)

    for d in range(1, NX):
        hello(dev(xx=xat(d)))
    for d in range(1, NY):
        hello(dev(yy=yat(d)))
    for d in range(1, NZ):
        hello(dev(ll=lax.rem(zl + d, NZ)))
    hello(dev(cc=1 - c))

    @pl.when(zh == 0)
    def _():
        for j in range(NZ):
            hello(dev(hh=1, ll=j))

    loads[0].wait()
    codes, count = [], jnp.int32(0)
    for p in range(16):
        live = jnp.where(lab[0, p] == 0, jnp.int32(1), jnp.int32(0))
        count = count + live
        codes.append(count * live)
    lane = iota((8, 128), 1)
    base = x * 32 + zh * 16
    mine = jnp.zeros((8, 128), F32)
    for p in range(16):
        mine = mine + jnp.where(lane == base + p, codes[p], 0).astype(F32)
    lx[0] = mine
    row, col = iota((16, 64), 0), iota((16, 64), 1)
    code_of = jnp.zeros((16, 64), jnp.int32)
    for p in range(16):
        code_of = code_of + jnp.where(col % 16 == p, codes[p], 0)
    pick = jnp.where((code_of > 0) & (row == (col // 16) * 4 + code_of - 1), 1.0, 0.0).astype(BF16)
    loads[1].wait()
    stacked = jnp.concatenate(
        [
            jnp.concatenate([t_in[:, j * 512 + g * 128 : j * 512 + g * 128 + 128] for j in range(NZ)], axis=1)
            for g in range(4)
        ],
        axis=0,
    )
    tiles = jnp.dot(pick, stacked, preferred_element_type=F32).astype(BF16)
    for j in range(NZ):
        tsend[j] = tiles[:, j * 128 : (j + 1) * 128]
    tx[0, x, zl] = tsend[zl]

    pl.semaphore_wait(barrier, jnp.where(zh == 0, 16, 22))

    @pl.when(zh == 1)
    def _():
        for j in range(NZ):
            pl.semaphore_signal(late_in, inc=1, device_id=dev(hh=0, ll=j), device_id_type=MESH)

    def label_x(d):
        return rc(lx.at[0], lx.at[d], lxs.at[d - 1], lxr.at[d - 1], dev(xx=xat(d)))

    for d in range(1, NX):
        label_x(d).start()

    def tile_near(j):
        return rc(tsend.at[j], tx.at[0, x, zl], tzs.at[0, j], tzr.at[0, zl], dev(ll=j))

    def tile_far(j):
        return rc(tsend.at[j], tx.at[1, x, zl], tzs.at[1, j], tzr.at[1, zl], dev(hh=1 - zh, ll=j))

    for j in range(NZ):

        @pl.when(zl != j)
        def _():
            tile_near(j).start()

    @pl.when(zh == 1)
    def _():
        for j in range(NZ):
            tile_far(j).start()

    for d in range(1, NX):
        label_x(d).wait_recv()
    ly[0] = (lx[0] + lx[1]) + (lx[2] + lx[3])

    def label_y(d):
        return rc(ly.at[0], ly.at[d], lys.at[d - 1], lyr.at[d - 1], dev(yy=yat(d)))

    for d in range(1, NY):
        label_y(d).start()

    def tile_wait(hi, j):
        rc(tsend.at[j], tx.at[hi, x, j], tzs.at[hi, j], tzr.at[hi, j], dev(ll=j)).wait_recv()

    def t_x(hi, d):
        return rc(tx.at[hi, x], tx.at[hi, x], txs.at[hi, d - 1], txr.at[hi, d - 1], dev(xx=xat(d)))

    def t_x_wait(hi, d):
        xo = xat(-d)
        rc(tx.at[hi, xo], tx.at[hi, xo], txs.at[hi, d - 1], txr.at[hi, d - 1], dev(xx=xo)).wait_recv()

    for j in range(NZ):

        @pl.when(zl != j)
        def _():
            tile_wait(0, j)

    for d in range(1, NX):
        t_x(0, d).start()

    for d in range(1, NY):
        label_y(d).wait_recv()
    rows8 = iota((8, 128), 0)
    plane = jnp.where(rows8 == y, ly[0], 0.0)
    for d in range(1, NY):
        plane = plane + jnp.where(rows8 == yat(-d), ly[d], 0.0)
    lz[0] = plane

    def compact(hi):
        ri, li = iota((16, 128), 0), iota((16, 128), 1)
        want = jnp.where(li // 32 == ri // 4, ri % 4 + 1, -1).astype(F32)
        parts = []
        for q in range(NY):
            block = jnp.where(jnp.broadcast_to(lz[hi, q : q + 1, :], (16, 128)) == want, 1.0, 0.0).astype(BF16)
            pieces = [block]
            if q:
                pieces.insert(0, jnp.zeros((16 * q, 128), BF16))
            if q < NY - 1:
                pieces.append(jnp.zeros((16 * (NY - 1 - q), 128), BF16))
            parts.append(jnp.concatenate(pieces, axis=0))
        select = jnp.concatenate(parts, axis=1)
        for sub in range(2):
            kept = lax.dot_general(
                v_in[sub * 256 : (sub + 1) * 256, :], select, (((1,), (1,)), ((), ())), preferred_element_type=F32
            )
            vb[zl, hi, sub] = kept.astype(BF16)
            v_send(0, hi, sub)

    def v_copy(way, k, hi, sub):
        slab = zl - k if way == 0 else zl + k
        here = vb.at[slab, hi, sub]
        return rc(
            here, here, vs.at[way, k, hi, sub], vr.at[way, k, hi, sub], dev(ll=zl + 1 if way == 0 else zl - 1)
        )

    def v_goes(way, k):
        return (zl >= k) & (zl < NZ - 1) if way == 0 else (zl + k < NZ) & (zl > 0)

    def v_send(k, hi, sub):
        for way in range(2):

            @pl.when(v_goes(way, k))
            def _():
                v_copy(way, k, hi, sub).start()

    def v_step(k, hi):
        for sub in range(2):
            for way in range(2):
                comes = zl >= k if way == 0 else zl + k < NZ

                @pl.when(comes)
                def _():
                    slab = zl - k if way == 0 else zl + k
                    here = vb.at[slab, hi, sub]
                    rc(
                        here, here, vs.at[way, k - 1, hi, sub], vr.at[way, k - 1, hi, sub],
                        dev(ll=zl - 1 if way == 0 else zl + 1),
                    ).wait_recv()

                if k < NZ - 1:

                    @pl.when(v_goes(way, k))
                    def _():
                        v_copy(way, k, hi, sub).start()

    def relayout(hi):
        i, j = iota((64, 64), 0), iota((64, 64), 1)
        perm = jnp.where(
            (i // 16 == (j // 4) % 4) & ((i // 4) % 4 == j // 16) & (i % 4 == j % 4), 1.0, 0.0
        ).astype(BF16)
        got = jnp.concatenate(
            [jnp.concatenate([tx[hi, xx, s] for xx in range(NX)], axis=0) for s in range(NZ)], axis=1
        )
        moved = jnp.dot(perm, got, preferred_element_type=F32).astype(BF16)
        for s in range(NZ):
            for g in range(4):
                ty[hi, y, s, :, g * 128 : (g + 1) * 128] = moved[g * 16 : (g + 1) * 16, s * 128 : (s + 1) * 128]

    def t_copy(hi, way, d, sub):
        here = ty.at[hi, yat(-d if way == 0 else d), pl.ds(3 * sub, 3)]
        return rc(here, here, tys.at[hi, way, d, sub], tyr.at[hi, way, d, sub], dev(yy=yat(1 if way == 0 else -1)))

    def t_goes(d, way, sub):
        return d < 3 or (d == 3 and sub == way)

    def t_step(hi, d):
        for sub in range(2):
            for way in range(2):
                if d > 0 and t_goes(d - 1, way, sub):
                    here = ty.at[hi, yat(-d if way == 0 else d), pl.ds(3 * sub, 3)]
                    rc(
                        here, here, tys.at[hi, way, d - 1, sub], tyr.at[hi, way, d - 1, sub],
                        dev(yy=yat(-1 if way == 0 else 1)),
                    ).wait_recv()
                if t_goes(d, way, sub):
                    t_copy(hi, way, d, sub).start()

    def multiply(s, first=False):
        right = jnp.concatenate([ty[hi, :, s].reshape(128, 512) for hi in range(2)], axis=0)
        for sub in range(2):
            left = jnp.concatenate([vb[s, 0, sub], vb[s, 1, sub]], axis=1)
            part = jnp.dot(left, right, preferred_element_type=F32)
            here = pl.ds(sub * 256, 256)
            acc[here, :] = part if first else acc[here, :] + part

    def multiply_at(k):
        @pl.when(zl >= k)
        def _():
            multiply(zl - k)

        @pl.when(zl + k < NZ)
        def _():
            multiply(zl + k)

    loads[2].wait()
    compact(0)
    v_step(1, 0)

    @pl.when(zh == 0)
    def _():
        pl.semaphore_wait(late_in, NZ)
        for j in range(NZ):
            tile_far(j).start()

    label_z = rc(lz.at[0], lz.at[1], lzs.at[0], lzs.at[1], dev(hh=1 - zh))
    label_z.start()

    for d in range(1, NX):
        t_x_wait(0, d)
    relayout(0)
    t_step(0, 0)
    v_step(2, 0)
    t_step(0, 1)
    for j in range(NZ):
        tile_wait(1, j)
    for d in range(1, NX):
        t_x(1, d).start()
    v_step(3, 0)
    t_step(0, 2)
    for d in range(1, NX):
        t_x_wait(1, d)
    relayout(1)
    t_step(1, 0)
    label_z.wait_recv()
    compact(1)
    v_step(4, 0)
    t_step(0, 3)
    t_step(1, 1)
    v_step(5, 0)
    t_step(0, 4)
    t_step(1, 2)
    v_step(1, 1)
    t_step(1, 3)
    v_step(2, 1)
    t_step(1, 4)

    loads[3].wait()
    loads[4].wait()
    loads[5].wait()
    for q in range(4):
        column = jnp.broadcast_to(abe[0:1, q * 128 : (q + 1) * 128], (128, 128)).T
        den[q * 128 : (q + 1) * 128, :] = jnp.concatenate([column, column], axis=1) - ije[...]
    multiply(zl, first=True)

    @pl.loop(1, 3)
    def _(k):
        multiply_at(k)

    for k in range(3, NZ):
        v_step(k, 1)

        @pl.loop(k, k + 1)
        def _(kk):
            multiply_at(kk)

    lo, hi_half = acc[:, :256], acc[:, 256:]
    xs[...] = jnp.where(c == 0, hi_half, lo).astype(BF16)
    swap = rc(xs, xr, cs.at[0], cs.at[1], dev(cc=1 - c))
    swap.start()
    own = jnp.where(c == 0, lo, hi_half) + res[...].astype(F32)
    swap.wait_recv()
    out_ref[...] = ((own + xr[...].astype(F32)) / den[...]).astype(BF16)

    swap.wait_send()
    label_z.wait_send()
    for d in range(1, NX):
        label_x(d).wait_send()
        t_x(0, d).wait_send()
        t_x(1, d).wait_send()
    for d in range(1, NY):
        label_y(d).wait_send()
    for j in range(NZ):

        @pl.when(zl != j)
        def _():
            tile_near(j).wait_send()

        tile_far(j).wait_send()
    for hi in range(2):
        for sub in range(2):
            for way in range(2):
                for d in range(4):
                    if t_goes(d, way, sub):
                        t_copy(hi, way, d, sub).wait_send()
                for k in range(NZ - 1):

                    @pl.when(v_goes(way, k))
                    def _():
                        v_copy(way, k, hi, sub).wait_send()


def local(integrals, amplitudes, cd_irrep, residual, ab_energy, ij_energy):
    anywhere = pl.BlockSpec(memory_space=pl.ANY)
    dma = pltpu.SemaphoreType.DMA
    return pl.pallas_call(
        kernel,
        out_shape=jax.ShapeDtypeStruct((512, 256), BF16),
        in_specs=[anywhere] * 6,
        out_specs=pl.BlockSpec(memory_space=pltpu.VMEM),
        scratch_shapes=[
            pltpu.SMEM((1, 16), jnp.int32),
            pltpu.VMEM((16, 3072), BF16),
            pltpu.VMEM((512, 1024), BF16),
            pltpu.VMEM((512, 256), BF16),
            pltpu.VMEM((1, 512), F32),
            pltpu.VMEM((1, 256), F32),
            pltpu.VMEM((512, 256), F32),
            pltpu.VMEM((NX, 8, 128), F32),
            pltpu.VMEM((NY, 8, 128), F32),
            pltpu.VMEM((2, 8, 128), F32),
            pltpu.VMEM((NZ, 16, 128), BF16),
            pltpu.VMEM((2, NX, NZ, 16, 128), BF16),
            pltpu.VMEM((2, NY, NZ, 16, 512), BF16),
            pltpu.VMEM((NZ, 2, 2, 256, 128), BF16),
            pltpu.VMEM((512, 512), F32),
            pltpu.VMEM((512, 256), BF16),
            pltpu.VMEM((512, 256), BF16),
            dma((6,)),
            dma((NX - 1,)),
            dma((NX - 1,)),
            dma((NY - 1,)),
            dma((NY - 1,)),
            dma((2,)),
            dma((2, NZ)),
            dma((2, NZ)),
            dma((2, NX - 1)),
            dma((2, NX - 1)),
            dma((2, 2, 4, 2)),
            dma((2, 2, 4, 2)),
            dma((2, NZ - 1, 2, 2)),
            dma((2, NZ - 1, 2, 2)),
            dma((2,)),
            pltpu.SemaphoreType.REGULAR,
        ],
        compiler_params=pltpu.CompilerParams(
            collective_id=0, has_side_effects=True, vmem_limit_bytes=56 * 1024 * 1024
        ),
        cost_estimate=pl.CostEstimate(flops=2 * 512 * 1536 * 512, bytes_accessed=2 << 20, transcendentals=0),
    )(
        integrals.reshape(512, 1024),
        amplitudes.reshape(16, 3072),
        cd_irrep,
        residual,
        ab_energy.reshape(1, 512),
        ij_energy.reshape(1, 256),
    )


def solution(mesh):
    return jax.shard_map(
        local,
        mesh=mesh,
        in_specs=(
            P("ab", "cd", None),
            P("cd", "ab", None),
            P("cd", "ab"),
            P("ab", "cd"),
            P("ab"),
            P("cd"),
        ),
        out_specs=P("ab", "cd"),
        check_vma=False,
    )
```

time: 325 us -> 68.5 us (0.21); the launches traced: 321 us -> 68.3 us
  waiting for transfers between devices: 295 us -> 0 us
  Pallas kernels: 0 us -> 66.7 us
  between operations: 13.4 us -> 0.01 us
  matrix products: 7.8 us -> 0 us
  other arithmetic: 3.45 us -> 0 us
    all_gather x1 -> x0, waiting for transfers between devices: 225 us -> none  [local(): lax.all_gather(masked, 'ab', axis=0, tiled=True)]
    reduce_scatter x1 -> x0, waiting for transfers between devices: 69.3 us -> none  [local(): lax.psum_scatter(slab_total.astype(jnp.bfloat16), 'cd', scatter_dimension...]
    pallas_call x0 -> x1, Pallas kernels: none -> 66.7 us  [local(): pl.pallas_call(kernel, out_shape=jax.ShapeDtypeStruct((512, 256), BF16),...]
    dot_general x1 -> x0, matrix products: 7.8 us -> none  [local(): jnp.dot(block, lax.all_gather(masked, 'ab', axis=0, tiled=True), preferre...]
  transfers between devices with their start and end apart: 2 -> 0, of which waited for: 2 -> 0; matrix products, arithmetic and copies ran while one was open for 0% -> 0% of each run, Pallas kernels for 0% -> 0%
where the time goes in v1:
time: 68.5 us; the launch traced here: 68.3 us
  Pallas kernels  66.7 us (97%)
  local copies, waits for them, and re-layouts  1.67 us (2%)
    pallas_call x1, Pallas kernels, local(): pl.pallas_call(kernel, out_shape=jax.ShapeDtypeStruct((512, 256), BF16),...  66.7 us
    unnamed x1, local copies, waits for them, and re-layouts  1.67 us

profile of v1, /device:TPU:1, one launch (start us, length us, event | category | flops | bytes accessed | tf_op | source)
XLA Modules:
  0.0 68.3 jit_solution(23127469451473972)
XLA Ops:
  0.0 66.7 %shard_map.64 = bf16[512,256]{1,0:T(8,128)(2,1)} custom-call(bf16[512,1024]{1,0:T(8,128)(2,1)} %bitcast.4, bf16[16,3072]{1,0:T(8,128)(2,1)} %bitcast.5, s32[1,16]{1,0:T(1,128)} %lab_hbm.1, bf16[512,256]{1,0:T(8,128)(2,1)} %res_hbm.1, f32[1,512]{1,0:T(1,128)} %bitcast.6, f32[1,256]{1,0:T(1,128)} %bitcast.7), custom_call_target="tpu_custom_call" | custom-call | flops 805306368 | bytes 2097152 | tf_op jit(solution)/shard_map/pallas_call | solution.py:372
  66.7 1.7 %copy.8 = bf16[512,256]{1,0:T(8,128)(2,1)} copy(bf16[512,256]{1,0:T(8,128)(2,1)} %shard_map.64) | data formatting | bytes 524288

commit v2 on v0

v2 whole, which is shorter than its diff:
```python
import jax
import jax.numpy as jnp
from jax import lax
from jax.experimental import pallas as pl
from jax.experimental.pallas import tpu as pltpu
from jax.sharding import PartitionSpec as P

MESH = pl.DeviceIdType.MESH
NX, NY, NZ = 4, 8, 6
NS = 4
ROWS = 512 // NS
F32, BF16 = jnp.float32, jnp.bfloat16


def iota(shape, dim):
    return lax.broadcasted_iota(jnp.int32, shape, dim)


def kernel(
    v_hbm, t_hbm, lab_hbm, res_hbm, ab_hbm, ij_hbm,
    out_hbm,
    lab, t_in, v_in, res, abe, ije, den,
    lx, ly, tsend, tz, tb, vb, acc, xs, xr, out,
    loc, lxs, lxr, lfs, lys, lyr, tzs, tzr, tys, tyr, txs, txr, vs, vr, cs, outs, in_near, in_far,
):
    ab, cd = lax.axis_index("ab"), lax.axis_index("cd")
    y, x, zh = ab // 8, (ab // 2) % 4, ab % 2
    zl, c = cd // 2, cd % 2

    def dev(yy=y, xx=x, hh=zh, ll=zl, cc=c):
        return ((yy * NX + xx) * 2 + hh, ll * 2 + cc)

    def rc(src, dst, ss, rs, to):
        return pltpu.make_async_remote_copy(
            src_ref=src, dst_ref=dst, send_sem=ss, recv_sem=rs, device_id=to, device_id_type=MESH
        )

    def xat(d):
        return lax.rem(x + d + NX, NX)

    def yat(d):
        return lax.rem(y + d + NY, NY)

    loads = [
        pltpu.make_async_copy(a, b, loc.at[i])
        for i, (a, b) in enumerate(
            [(lab_hbm, lab), (t_hbm, t_in), (v_hbm, v_in), (res_hbm, res), (ab_hbm, abe), (ij_hbm, ije)]
        )
    ]
    for cp in loads:
        cp.start()

    barrier = pltpu.get_barrier_semaphore()

    def signal(sem, to):
        pl.semaphore_signal(sem, inc=1, device_id=to, device_id_type=MESH)

    for d in range(1, NX):
        signal(barrier, dev(xx=xat(d)))
    for d in range(1, NY):
        signal(barrier, dev(yy=yat(d)))
    signal(barrier, dev(cc=1 - c))

    @pl.when(zl > 0)
    def _():
        signal(barrier, dev(ll=zl - 1))

    for j in range(1, NZ):

        @pl.when(j > zl)
        def _():
            signal(barrier, dev(ll=j))

    def signal_other_half(sem):
        for j in range(NZ):
            signal(sem, dev(hh=1 - zh, ll=j))
        for d in range(1, NX):
            signal(sem, dev(hh=1 - zh, xx=xat(d)))

    @pl.when(zh == 0)
    def _():
        signal_other_half(barrier)

    loads[0].wait()
    codes, count = [], jnp.int32(0)
    for p in range(16):
        live = jnp.where(lab[0, p] == 0, jnp.int32(1), jnp.int32(0))
        count = count + live
        codes.append(count * live)
    lane = iota((1, 128), 1)
    base = x * 32 + zh * 16
    mine = jnp.zeros((1, 128), F32)
    for p in range(16):
        mine = mine + jnp.where(lane == base + p, codes[p], 0).astype(F32)
    lx[0, 0] = mine
    row, col = iota((16, 64), 0), iota((16, 64), 1)
    code_of = jnp.zeros((16, 64), jnp.int32)
    for p in range(16):
        code_of = code_of + jnp.where(col % 16 == p, codes[p], 0)
    pick = jnp.where((code_of > 0) & (row == (col // 16) * 4 + code_of - 1), 1.0, 0.0).astype(BF16)
    loads[1].wait()
    stacked = jnp.concatenate(
        [
            jnp.concatenate([t_in[:, j * 512 + g * 128 : j * 512 + g * 128 + 128] for j in range(NZ)], axis=1)
            for g in range(4)
        ],
        axis=0,
    )
    tiles = jnp.dot(pick, stacked, preferred_element_type=F32).astype(BF16)
    for j in range(NZ):
        tsend[j] = tiles[:, j * 128 : (j + 1) * 128]
    tz[0, y, zl] = tsend[zl]

    def label_x(d):
        return rc(lx.at[0, 0], lx.at[0, d], lxs.at[d - 1], lxr.at[0, d], dev(xx=xat(d)))

    def label_far(d):
        return rc(lx.at[0, 0], lx.at[1, d], lfs.at[d], lxr.at[1, d], dev(hh=1 - zh, xx=xat(d)))

    def label_y(hi, d):
        here = ly.at[hi, y]
        return rc(here, here, lys.at[hi, d - 1], lyr.at[hi, d - 1], dev(yy=yat(d)))

    def label_y_wait(hi, d):
        here = ly.at[hi, yat(-d)]
        rc(here, here, lys.at[hi, d - 1], lyr.at[hi, d - 1], dev(yy=yat(-d))).wait_recv()

    def tile_near(j):
        return rc(tsend.at[j], tz.at[0, y, zl], tzs.at[0, j], tzr.at[0, zl], dev(ll=j))

    def tile_far(j):
        return rc(tsend.at[j], tz.at[1, y, zl], tzs.at[1, j], tzr.at[1, zl], dev(hh=1 - zh, ll=j))

    def tile_wait(hi, j):
        rc(tsend.at[j], tz.at[hi, y, j], tzs.at[hi, j], tzr.at[hi, j], dev(ll=j)).wait_recv()

    def t_y(hi, d):
        here = tz.at[hi, y]
        return rc(here, here, tys.at[hi, d - 1], tyr.at[hi, d - 1], dev(yy=yat(d)))

    def t_y_wait(hi, d):
        here = tz.at[hi, yat(-d)]
        rc(here, here, tys.at[hi, d - 1], tyr.at[hi, d - 1], dev(yy=yat(-d))).wait_recv()

    def relayout(hi):
        i, j = iota((128, 128), 0), iota((128, 128), 1)
        perm = jnp.where(
            (i // 32 == (j // 4) % 4) & ((i // 4) % 8 == j // 16) & (i % 4 == j % 4), 1.0, 0.0
        ).astype(BF16)
        got = jnp.concatenate([tz[hi, :, s].reshape(128, 128) for s in range(NZ)], axis=1)
        moved = jnp.dot(perm, got, preferred_element_type=F32).astype(BF16)
        for s in range(NZ):
            for g in range(4):
                tb[hi, x, s, :, g * 128 : (g + 1) * 128] = moved[g * 32 : (g + 1) * 32, s * 128 : (s + 1) * 128]

    def t_x(hi, way, sub):
        here = tb.at[hi, x, pl.ds(3 * sub, 3)]
        return rc(here, here, txs.at[hi, way, sub], txr.at[hi, way, sub], dev(xx=xat(1 - 2 * way)))

    def t_x_wait(hi, way, sub):
        here = tb.at[hi, xat(2 * way - 1), pl.ds(3 * sub, 3)]
        rc(here, here, txs.at[hi, way, sub], txr.at[hi, way, sub], dev(xx=xat(2 * way - 1))).wait_recv()

    def t_x_on(hi, way):
        here = tb.at[hi, xat(2 * way - 1), pl.ds(3 * way, 3)]
        return rc(here, here, txs.at[hi, way, 2], txr.at[hi, way, 2], dev(xx=xat(1 - 2 * way)))

    def t_x_start(hi):
        for k in range(2):
            for way in range(2):
                t_x(hi, way, (way + k) % 2).start()

    def t_x_relay(hi):
        for way in range(2):
            t_x_wait(hi, way, way)
            t_x_on(hi, way).start()

    def t_x_end(hi):
        for way in range(2):
            t_x_wait(hi, way, 1 - way)
            here = tb.at[hi, xat(2), pl.ds(3 * way, 3)]
            rc(here, here, txs.at[hi, way, 2], txr.at[hi, way, 2], dev(xx=xat(2 * way - 1))).wait_recv()

    def v_out(way, k, hi, sub):
        here = vb.at[zl - k if way == 0 else zl + k, hi, sub]
        return rc(
            here, here, vs.at[way, k, hi, sub], vr.at[way, k, hi, sub], dev(ll=zl + 1 if way == 0 else zl - 1)
        )

    def v_goes(way, k):
        return (zl >= k) & (zl < NZ - 1) if way == 0 else (zl + k < NZ) & (zl > 0)

    def v_comes(way, k):
        return zl >= k if way == 0 else zl + k < NZ

    def v_arrive(k, hi, sub):
        for way in range(2):

            @pl.when(v_comes(way, k))
            def _():
                here = vb.at[zl - k if way == 0 else zl + k, hi, sub]
                rc(
                    here, here, vs.at[way, k - 1, hi, sub], vr.at[way, k - 1, hi, sub],
                    dev(ll=zl - 1 if way == 0 else zl + 1),
                ).wait_recv()

            if k < NZ - 1:

                @pl.when(v_goes(way, k))
                def _():
                    v_out(way, k, hi, sub).start()

    def v_step(k, hi):
        for sub in range(NS):
            v_arrive(k, hi, sub)

    def compact(hi):
        ri, li = iota((128, 128), 0), iota((128, 128), 1)
        want = jnp.where(li // 32 == ri // 32, ri % 4 + 1, -1)
        parts = []
        for q in range(NY):
            mark = jnp.where((ri // 4) % 8 == q, want, -1).astype(F32)
            parts.append(jnp.where(jnp.broadcast_to(ly[hi, q], (128, 128)) == mark, 1.0, 0.0).astype(BF16))
        select = jnp.concatenate(parts, axis=1)
        for sub in range(NS):
            kept = lax.dot_general(
                v_in[sub * ROWS : (sub + 1) * ROWS, :], select, (((1,), (1,)), ((), ())), preferred_element_type=F32
            )
            vb[zl, hi, sub] = kept.astype(BF16)
            for way in range(2):

                @pl.when(v_goes(way, 0))
                def _():
                    v_out(way, 0, hi, sub).start()

    def right_of(s, hi):
        return tb[hi, :, s].reshape(128, 512)

    def multiply(s, first=False):
        right = jnp.concatenate([right_of(s, 0), right_of(s, 1)], axis=0)
        for sub in range(NS):
            left = jnp.concatenate([vb[s, 0, sub], vb[s, 1, sub]], axis=1)
            part = jnp.dot(left, right, preferred_element_type=F32)
            here = pl.ds(sub * ROWS, ROWS)
            acc[here, :] = part if first else acc[here, :] + part

    def multiply_at(k):
        @pl.when(zl >= k)
        def _():
            multiply(zl - k)

        @pl.when(zl + k < NZ)
        def _():
            multiply(zl + k)

    far = jnp.where(zl == 0, NZ - 1, 0)

    def multiply_last(hi, sub):
        @pl.when((zl == 0) | (zl == NZ - 1))
        def _():
            here = pl.ds(sub * ROWS, ROWS)
            acc[here, :] += jnp.dot(vb[far, hi, sub], right_of(far, hi), preferred_element_type=F32)

    pl.semaphore_wait(barrier, 11 + zl + zh * 9 + jnp.where(zl < NZ - 1, 1, 0))
    for d in range(1, NX):
        label_x(d).start()

    @pl.when(zh == 1)
    def _():
        signal_other_half(in_far)
        for d in range(NX):
            label_far(d).start()
        for j in range(NZ):
            tile_far(j).start()

    for j in range(NZ - 1):

        @pl.when(zl > j)
        def _():
            signal(in_near, dev(ll=j))
            tile_near(j).start()

    for d in range(1, NX):
        label_x(d).wait_recv()
    ly[0, y] = (lx[0, 0] + lx[0, 1]) + (lx[0, 2] + lx[0, 3])
    for d in range(1, NY):
        label_y(0, d).start()
    for d in range(1, NY):
        label_y_wait(0, d)
    loads[2].wait()
    compact(0)

    @pl.when(zl < NZ - 1)
    def _():
        pl.semaphore_wait(in_near, NZ - 1 - zl)

    for j in range(1, NZ):

        @pl.when(zl < j)
        def _():
            tile_near(j).start()

    for j in range(NZ):

        @pl.when(zl != j)
        def _():
            tile_wait(0, j)

    for d in range(1, NY):
        t_y(0, d).start()
    v_step(1, 0)

    @pl.when(zh == 0)
    def _():
        pl.semaphore_wait(in_far, 9)
        for d in range(NX):
            label_far(d).start()
        for j in range(NZ):
            tile_far(j).start()

    for j in range(NZ):
        tile_wait(1, j)
    for d in range(1, NY):
        t_y(1, d).start()
    for d in range(NX):
        rc(lx.at[0, 0], lx.at[1, d], lfs.at[d], lxr.at[1, d], dev(hh=1 - zh, xx=xat(d))).wait_recv()
    ly[1, y] = (lx[1, 0] + lx[1, 1]) + (lx[1, 2] + lx[1, 3])
    for d in range(1, NY):
        label_y(1, d).start()
    v_step(2, 0)
    for d in range(1, NY):
        t_y_wait(0, d)
    relayout(0)
    t_x_start(0)
    for d in range(1, NY):
        label_y_wait(1, d)
    compact(1)
    v_step(3, 0)
    for d in range(1, NY):
        t_y_wait(1, d)
    relayout(1)
    t_x_start(1)
    v_step(1, 1)
    t_x_relay(0)
    v_step(4, 0)
    v_step(2, 1)
    t_x_relay(1)
    v_step(5, 0)
    t_x_end(0)
    v_step(3, 1)
    t_x_end(1)

    loads[3].wait()
    loads[4].wait()
    loads[5].wait()
    for q in range(4):
        column = jnp.broadcast_to(abe[0:1, q * 128 : (q + 1) * 128], (128, 128)).T
        den[q * 128 : (q + 1) * 128, :] = jnp.concatenate([column, column], axis=1) - ije[...]
    multiply(zl, first=True)

    @pl.loop(1, 4)
    def _(k):
        multiply_at(k)

    v_step(4, 1)

    @pl.loop(4, 5)
    def _(k):
        multiply_at(k)

    for sub in range(NS):
        multiply_last(0, sub)

    def swap(sub):
        here = pl.ds(sub * ROWS, ROWS)
        return rc(xs.at[here], xr.at[here], cs.at[0, sub], cs.at[1, sub], dev(cc=1 - c))

    def put(sub):
        here = pl.ds(sub * ROWS, ROWS)
        return pltpu.make_async_copy(out.at[here], out_hbm.at[here], outs.at[sub])

    for sub in range(NS):
        v_arrive(NZ - 1, 1, sub)
        multiply_last(1, sub)
        here = pl.ds(sub * ROWS, ROWS)
        xs[here, :] = jnp.where(c == 0, acc[here, 256:], acc[here, :256]).astype(BF16)
        swap(sub).start()
    for sub in range(NS):
        here = pl.ds(sub * ROWS, ROWS)
        own = jnp.where(c == 0, acc[here, :256], acc[here, 256:]) + res[here, :].astype(F32)
        swap(sub).wait_recv()
        out[here, :] = ((own + xr[here, :].astype(F32)) / den[here, :]).astype(BF16)
        put(sub).start()

    for d in range(1, NX):
        label_x(d).wait_send()
    for d in range(NX):
        label_far(d).wait_send()
    for j in range(NZ):

        @pl.when(zl != j)
        def _():
            tile_near(j).wait_send()

        tile_far(j).wait_send()
    for hi in range(2):
        for d in range(1, NY):
            label_y(hi, d).wait_send()
            t_y(hi, d).wait_send()
        for way in range(2):
            t_x(hi, way, 0).wait_send()
            t_x(hi, way, 1).wait_send()
            t_x_on(hi, way).wait_send()
        for sub in range(NS):
            for way in range(2):
                for k in range(NZ - 1):

                    @pl.when(v_goes(way, k))
                    def _():
                        v_out(way, k, hi, sub).wait_send()

    for sub in range(NS):
        swap(sub).wait_send()
        put(sub).wait()


def local(integrals, amplitudes, cd_irrep, residual, ab_energy, ij_energy):
    anywhere = pl.BlockSpec(memory_space=pl.ANY)
    dma = pltpu.SemaphoreType.DMA
    return pl.pallas_call(
        kernel,
        out_shape=jax.ShapeDtypeStruct((512, 256), BF16),
        in_specs=[anywhere] * 6,
        out_specs=anywhere,
        scratch_shapes=[
            pltpu.SMEM((1, 16), jnp.int32),
            pltpu.VMEM((16, 3072), BF16),
            pltpu.VMEM((512, 1024), BF16),
            pltpu.VMEM((512, 256), BF16),
            pltpu.VMEM((1, 512), F32),
            pltpu.VMEM((1, 256), F32),
            pltpu.VMEM((512, 256), F32),
            pltpu.VMEM((2, NX, 1, 128), F32),
            pltpu.VMEM((2, NY, 1, 128), F32),
            pltpu.VMEM((NZ, 16, 128), BF16),
            pltpu.VMEM((2, NY, NZ, 16, 128), BF16),
            pltpu.VMEM((2, NX, NZ, 32, 512), BF16),
            pltpu.VMEM((NZ, 2, NS, ROWS, 128), BF16),
            pltpu.VMEM((512, 512), F32),
            pltpu.VMEM((512, 256), BF16),
            pltpu.VMEM((512, 256), BF16),
            pltpu.VMEM((512, 256), BF16),
            dma((6,)),
            dma((NX - 1,)),
            dma((2, NX)),
            dma((NX,)),
            dma((2, NY - 1)),
            dma((2, NY - 1)),
            dma((2, NZ)),
            dma((2, NZ)),
            dma((2, NY - 1)),
            dma((2, NY - 1)),
            dma((2, 2, 3)),
            dma((2, 2, 3)),
            dma((2, NZ - 1, 2, NS)),
            dma((2, NZ - 1, 2, NS)),
            dma((2, NS)),
            dma((NS,)),
            pltpu.SemaphoreType.REGULAR,
            pltpu.SemaphoreType.REGULAR,
        ],
        compiler_params=pltpu.CompilerParams(
            collective_id=0, has_side_effects=True, vmem_limit_bytes=56 * 1024 * 1024
        ),
        cost_estimate=pl.CostEstimate(flops=2 * 512 * 1536 * 512, bytes_accessed=2 << 20, transcendentals=0),
    )(
        integrals.reshape(512, 1024),
        amplitudes.reshape(16, 3072),
        cd_irrep,
        residual,
        ab_energy.reshape(1, 512),
        ij_energy.reshape(1, 256),
    )


def solution(mesh):
    return jax.shard_map(
        local,
        mesh=mesh,
        in_specs=(
            P("ab", "cd", None),
            P("cd", "ab", None),
            P("cd", "ab"),
            P("ab", "cd"),
            P("ab"),
            P("cd"),
        ),
        out_specs=P("ab", "cd"),
        check_vma=False,
    )
```

time: 325 us -> 60.2 us (0.19); the launches traced: 321 us -> 60 us
  waiting for transfers between devices: 295 us -> 0 us
  Pallas kernels: 0 us -> 58.3 us
  between operations: 13.4 us -> 0.01 us
  matrix products: 7.8 us -> 0 us
  other arithmetic: 3.45 us -> 0 us
    all_gather x1 -> x0, waiting for transfers between devices: 225 us -> none  [local(): lax.all_gather(masked, 'ab', axis=0, tiled=True)]
    reduce_scatter x1 -> x0, waiting for transfers between devices: 69.3 us -> none  [local(): lax.psum_scatter(slab_total.astype(jnp.bfloat16), 'cd', scatter_dimension...]
    pallas_call x0 -> x1, Pallas kernels: none -> 58.3 us  [local(): pl.pallas_call(kernel, out_shape=jax.ShapeDtypeStruct((512, 256), BF16),...]
    dot_general x1 -> x0, matrix products: 7.8 us -> none  [local(): jnp.dot(block, lax.all_gather(masked, 'ab', axis=0, tiled=True), preferre...]
  transfers between devices with their start and end apart: 2 -> 0, of which waited for: 2 -> 0; matrix products, arithmetic and copies ran while one was open for 0% -> 0% of each run, Pallas kernels for 0% -> 0%
where the time goes in v2:
time: 60.2 us; the launch traced here: 60 us
  Pallas kernels  58.3 us (97%)
  local copies, waits for them, and re-layouts  1.67 us (3%)
    pallas_call x1, Pallas kernels, local(): pl.pallas_call(kernel, out_shape=jax.ShapeDtypeStruct((512, 256), BF16),...  58.3 us
    unnamed x1, local copies, waits for them, and re-layouts  1.67 us

profile of v2, /device:TPU:1, one launch (start us, length us, event | category | flops | bytes accessed | tf_op | source)
XLA Modules:
  0.0 60.0 jit_solution(49321093923873726)
XLA Ops:
  0.0 58.3 %shard_map.64 = bf16[512,256]{1,0:T(8,128)(2,1)} custom-call(bf16[512,1024]{1,0:T(8,128)(2,1)} %bitcast.4, bf16[16,3072]{1,0:T(8,128)(2,1)} %bitcast.5, s32[1,16]{1,0:T(1,128)} %lab_hbm.1, bf16[512,256]{1,0:T(8,128)(2,1)} %res_hbm.1, f32[1,512]{1,0:T(1,128)} %bitcast.6, f32[1,256]{1,0:T(1,128)} %bitcast.7), custom_call_target="tpu_custom_call" | custom-call | flops 805306368 | bytes 2097152 | tf_op jit(solution)/shard_map/pallas_call | solution.py:430
  58.3 1.7 %copy.8 = bf16[512,256]{1,0:T(8,128)(2,1)} copy(bf16[512,256]{1,0:T(8,128)(2,1)} %shard_map.64) | data formatting | bytes 524288

commit v3 on v2

--- a/solution.py
+++ b/solution.py
@@ -290,6 +290,13 @@
     loads[2].wait()
     compact(0)
 
+    loads[3].wait()
+    loads[4].wait()
+    loads[5].wait()
+    for q in range(4):
+        column = jnp.broadcast_to(abe[0:1, q * 128 : (q + 1) * 128], (128, 128)).T
+        den[q * 128 : (q + 1) * 128, :] = jnp.concatenate([column, column], axis=1) - ije[...]
+
     @pl.when(zl < NZ - 1)
     def _():
         pl.semaphore_wait(in_near, NZ - 1 - zl)
@@ -318,15 +325,15 @@
         for j in range(NZ):
             tile_far(j).start()
 
-    for j in range(NZ):
-        tile_wait(1, j)
-    for d in range(1, NY):
-        t_y(1, d).start()
     for d in range(NX):
         rc(lx.at[0, 0], lx.at[1, d], lfs.at[d], lxr.at[1, d], dev(hh=1 - zh, xx=xat(d))).wait_recv()
     ly[1, y] = (lx[1, 0] + lx[1, 1]) + (lx[1, 2] + lx[1, 3])
     for d in range(1, NY):
         label_y(1, d).start()
+    for j in range(NZ):
+        tile_wait(1, j)
+    for d in range(1, NY):
+        t_y(1, d).start()
     v_step(2, 0)
     for d in range(1, NY):
         t_y_wait(0, d)
@@ -346,25 +353,14 @@
     v_step(2, 1)
     t_x_relay(1)
     v_step(5, 0)
+    v_step(3, 1)
+    v_step(4, 1)
     t_x_end(0)
-    v_step(3, 1)
     t_x_end(1)
 
-    loads[3].wait()
-    loads[4].wait()
-    loads[5].wait()
-    for q in range(4):
-        column = jnp.broadcast_to(abe[0:1, q * 128 : (q + 1) * 128], (128, 128)).T
-        den[q * 128 : (q + 1) * 128, :] = jnp.concatenate([column, column], axis=1) - ije[...]
     multiply(zl, first=True)
 
-    @pl.loop(1, 4)
-    def _(k):
-        multiply_at(k)
-
-    v_step(4, 1)
-
-    @pl.loop(4, 5)
+    @pl.loop(1, NZ - 1)
     def _(k):
         multiply_at(k)
 

time: 60.2 us -> 58.6 us (0.973)
  Pallas kernels: 58.3 us -> 56.7 us
    pallas_call x1, Pallas kernels: 58.3 us -> 56.7 us  [local(): pl.pallas_call(kernel, out_shape=jax.ShapeDtypeStruct((512, 256), BF16),...]
where the time goes in v3:
time: 58.6 us; the launch traced here: 58.4 us
  Pallas kernels  56.7 us (97%)
  local copies, waits for them, and re-layouts  1.67 us (3%)
    pallas_call x1, Pallas kernels, local(): pl.pallas_call(kernel, out_shape=jax.ShapeDtypeStruct((512, 256), BF16),...  56.7 us
    unnamed x1, local copies, waits for them, and re-layouts  1.67 us

profile of v3, /device:TPU:1, one launch (start us, length us, event | category | flops | bytes accessed | tf_op | source)
XLA Modules:
  0.0 58.4 jit_solution(3914933221781990473)
XLA Ops:
  0.0 56.7 %shard_map.64 = bf16[512,256]{1,0:T(8,128)(2,1)} custom-call(bf16[512,1024]{1,0:T(8,128)(2,1)} %bitcast.4, bf16[16,3072]{1,0:T(8,128)(2,1)} %bitcast.5, s32[1,16]{1,0:T(1,128)} %lab_hbm.1, bf16[512,256]{1,0:T(8,128)(2,1)} %res_hbm.1, f32[1,512]{1,0:T(1,128)} %bitcast.6, f32[1,256]{1,0:T(1,128)} %bitcast.7), custom_call_target="tpu_custom_call" | custom-call | flops 805306368 | bytes 2097152 | tf_op jit(solution)/shard_map/pallas_call | solution.py:426
  56.7 1.7 %copy.8 = bf16[512,256]{1,0:T(8,128)(2,1)} copy(bf16[512,256]{1,0:T(8,128)(2,1)} %shard_map.64) | data formatting | bytes 524288
